TPU v7x, 32 devices: a whole 2x2x4 slice. The times are simulated.
32 devices in a mesh: section: 2 (over x), dp: 16 (over z, y, core).
Axes of the slice: x: 2, y: 2, z: 4, core: 2. Of those that a mesh axis runs over, the one named last changes fastest.
Arguments:
- entering_tokens: bfloat16 [4, 16, 256, 384], P(None, 'dp'), may hold values from -6 to 6
- output_sensitivity: bfloat16 [4, 16, 256, 384], P(None, 'dp'), may hold values from -6 to 6
- picture_tile_extents: int32 [4, 16, 2], P(None, 'dp'), may hold values from 8 to 16
- pointwise_enlarge: bfloat16 [384, 1536], replicated, may hold values from -0.3125 to 0.3125
- enlarge_bias: float32 [1536], replicated, may hold values from -3 to 3
- channelwise_kernel: float32 [9, 1536], replicated, may hold values from -2 to 2
- channelwise_conv_bias: float32 [1536], replicated, may hold values from -3 to 3
- pointwise_contract: bfloat16 [1536, 384], replicated, may hold values from -0.15625 to 0.15625
- convblock_scale: float32 [384], replicated, may hold values from 0.1 to 1.9
- convblock_offset: float32 [384], replicated, may hold values from -3 to 3
- attend_scale: float32 [384], replicated, may hold values from 0.1 to 1.9
- attend_offset: float32 [384], replicated, may hold values from -3 to 3
- query_key_proj: bfloat16 [384, 1152], replicated, may hold values from -0.3125 to 0.3125
- heads_output_proj: bfloat16 [384, 384], replicated, may hold values from -3.5 to 3.5
- heads_output_bias: float32 [384], replicated, may hold values from -3 to 3
- feedforward_scale: float32 [384], replicated, may hold values from 0.1 to 1.9
- feedforward_offset: float32 [384], replicated, may hold values from -3 to 3
- feedforward_enlarge: bfloat16 [384, 1536], replicated, may hold values from -0.3125 to 0.3125
- feedforward_enlarge_bias: float32 [1536], replicated, may hold values from -3 to 3
- feedforward_contract: bfloat16 [1536, 384], replicated, may hold values from -0.15625 to 0.15625
- contract_bias: float32 [384], replicated, may hold values from -3 to 3
Outputs:
- section_ends: bfloat16 [2, 4, 16, 256, 384], P('section', None, 'dp')
- root_means: float32 [2, 4, 16], P('section', None, 'dp')
- expander_grad: float32 [384, 1536], replicated
- upshift_grad: float32 [1536], replicated
- depthwise_grad: float32 [9, 1536], replicated
- depthshift_grad: float32 [1536], replicated
- projector_grad: float32 [1536, 384], replicated
- postgain_grad: float32 [384], replicated
- postshift_grad: float32 [384], replicated
- pregain_grad: float32 [384], replicated
- preshift_grad: float32 [384], replicated
- attention_grad: float32 [384, 1152], replicated
- mixing_grad: float32 [384, 384], replicated
- mixshift_grad: float32 [384], replicated
- midgain_grad: float32 [384], replicated
- midshift_grad: float32 [384], replicated
- widener_grad: float32 [384, 1536], replicated
- wideshift_grad: float32 [1536], replicated
- narrower_grad: float32 [1536, 384], replicated
- narrowshift_grad: float32 [384], replicated
Inputs may be any that keep to these rules, and one draw needn't show every extreme that they name: Image (m, i) occupies the slots of the first picture_tile_extents[m, i, 0] rows and first picture_tile_extents[m, i, 1] columns of its 16 x 16 grid.
All inputs are finite; a program needn't handle non-finite values.
Results may differ from a plain program's by a relative error of at most 0.015.
Values may be sent and summed in bfloat16 or wider, within the bound.
No kernel may reach another device: no remote copies, remote signals or barrier semaphores. Data moves between devices by JAX's collectives and lax.ppermute only.
A program may use at most 256 MiB of HBM per device.

v0:
```python
import math

import jax
import jax.numpy as jnp
from jax import lax
from jax.sharding import PartitionSpec as P

HEADS = 6
SIDE = 16


EPSILON = 1e-05
BLOCKED = -1000000000.0


def passed_along(value, axis, steps):
    count = lax.axis_size(axis)
    first, last = (max(0, -steps), min(count, count - steps))
    return lax.ppermute(value, axis, [(source, source + steps) for source in range(first, last)])


def grid_mask(picture_tile_extents):
    places = jnp.arange(SIDE, dtype=jnp.int32)
    inside = (places[None, :, None] < picture_tile_extents[:, 0, None, None]) & (
        places[None, None, :] < picture_tile_extents[:, 1, None, None]
    )
    return inside.reshape(picture_tile_extents.shape[0], SIDE * SIDE).astype(jnp.float32)


def norm_ahead_pass(values, norm_gain, norm_shift):
    centered = values - jnp.mean(values, axis=-1, keepdims=True)
    inverse = lax.rsqrt(jnp.mean(centered * centered, axis=-1, keepdims=True) + EPSILON)
    scaled = centered * inverse
    return (scaled * norm_gain + norm_shift, scaled, inverse)


def norm_reverse_pass(upstream, scaled, inverse, norm_gain):
    lifted = upstream * norm_gain
    inner = (
        lifted
        - jnp.mean(lifted, axis=-1, keepdims=True)
        - scaled * jnp.mean(lifted * scaled, axis=-1, keepdims=True)
    )
    return (inverse * inner, jnp.sum(upstream * scaled, axis=0), jnp.sum(upstream, axis=0))


def product(left, right):
    return jnp.dot(left, right, preferred_element_type=jnp.float32)


def left_product(left, right):
    return jnp.einsum("na,nb->ab", left, right, preferred_element_type=jnp.float32)


def right_product(left, right):
    return jnp.einsum("na,ba->nb", left, right, preferred_element_type=jnp.float32)


def root_mean(values, valid):
    squares = jnp.sum(values * values * valid[:, :, None], axis=(1, 2))
    return jnp.sqrt(squares / (jnp.sum(valid, axis=1) * values.shape[2]))


def expand_forward(
    local_in,
    valid,
    pointwise_enlarge,
    enlarge_bias,
    channelwise_kernel,
    channelwise_conv_bias,
    pointwise_contract,
    convblock_scale,
    convblock_offset,
):
    images, slots, width = local_in.shape
    channels = pointwise_enlarge.shape[1]
    unrolled_entries = local_in.reshape(-1, width)
    expanded = product(unrolled_entries, pointwise_enlarge) + enlarge_bias
    grid_cells = expanded.reshape(images, SIDE, SIDE, channels) * valid.reshape(
        images, SIDE, SIDE, 1
    )
    padded = jnp.pad(grid_cells, ((0, 0), (1, 1), (1, 1), (0, 0)))
    convolved = channelwise_conv_bias + jnp.zeros_like(grid_cells)
    for tap_index in range(9):
        row_off = tap_index // 3
        col_off = tap_index % 3
        convolved = (
            convolved
            + padded[:, row_off : row_off + SIDE, col_off : col_off + SIDE, :]
            * channelwise_kernel[tap_index]
        )
    active = jax.nn.silu(convolved).astype(jnp.bfloat16).reshape(-1, channels)
    projected = product(active, pointwise_contract)
    standardized_entries, scaled, inverse = norm_ahead_pass(
        projected, convblock_scale, convblock_offset
    )
    sent = (
        (unrolled_entries.astype(jnp.float32) + standardized_entries)
        .astype(jnp.bfloat16)
        .reshape(images, slots, width)
    )
    return (sent, (padded, convolved, active, scaled, inverse))


def expand_skip(local_in, channels):
    images, slots, width = local_in.shape
    rows_all = images * slots
    return (
        jnp.zeros((images, slots, width), jnp.bfloat16),
        (
            jnp.zeros((images, SIDE + 2, SIDE + 2, channels), jnp.float32),
            jnp.zeros((images, SIDE, SIDE, channels), jnp.float32),
            jnp.zeros((rows_all, channels), jnp.bfloat16),
            jnp.zeros((rows_all, width), jnp.float32),
            jnp.zeros((rows_all, 1), jnp.float32),
        ),
    )


def expand_backward(
    local_in,
    valid,
    kept,
    returned,
    pointwise_enlarge,
    channelwise_kernel,
    pointwise_contract,
    convblock_scale,
):
    padded, convolved, active, scaled, inverse = kept
    images, slots, width = local_in.shape
    channels = pointwise_enlarge.shape[1]
    incoming = returned.reshape(-1, width).astype(jnp.float32)
    grad_proj, grad_postgain, grad_postshift = norm_reverse_pass(
        incoming, scaled, inverse, convblock_scale
    )
    proj_low = grad_proj.astype(jnp.bfloat16)
    grad_projector = left_product(active, proj_low)
    grad_active = right_product(proj_low, pointwise_contract).reshape(images, SIDE, SIDE, channels)
    sigmoid_of = jax.nn.sigmoid(convolved)
    grad_conv = grad_active * sigmoid_of * (1.0 + convolved * (1.0 - sigmoid_of))
    grad_depthshift = jnp.sum(grad_conv, axis=(0, 1, 2))
    padded_grad = jnp.pad(grad_conv, ((0, 0), (1, 1), (1, 1), (0, 0)))
    kernel_rows = []
    grad_grid = jnp.zeros_like(grad_conv)
    for tap_index in range(9):
        row_off = tap_index // 3
        col_off = tap_index % 3
        kernel_rows.append(
            jnp.sum(
                padded[:, row_off : row_off + SIDE, col_off : col_off + SIDE, :] * grad_conv,
                axis=(0, 1, 2),
            )
        )
        grad_grid = (
            grad_grid
            + padded_grad[:, 2 - row_off : 2 - row_off + SIDE, 2 - col_off : 2 - col_off + SIDE, :]
            * channelwise_kernel[tap_index]
        )
    grad_expanded = (grad_grid * valid.reshape(images, SIDE, SIDE, 1)).reshape(-1, channels)
    grad_upshift = jnp.sum(grad_expanded, axis=0)
    expanded_low = grad_expanded.astype(jnp.bfloat16)
    grad_expander = left_product(local_in.reshape(-1, width), expanded_low)
    grad_values = (incoming + right_product(expanded_low, pointwise_enlarge)).reshape(
        images, slots, width
    )
    grads_one = (
        grad_expander,
        grad_upshift,
        jnp.stack(kernel_rows),
        grad_depthshift,
        grad_projector,
        grad_postgain,
        grad_postshift,
    )
    return (grad_values.astype(jnp.bfloat16), root_mean(grad_values, valid), grads_one)


def expand_back_skip(local_in, templates):
    images, slots, width = local_in.shape
    return (
        jnp.zeros((images, slots, width), jnp.bfloat16),
        jnp.zeros((images,), jnp.float32),
        tuple((jnp.zeros(template.shape, jnp.float32) for template in templates)),
    )


def block_pass(
    arrived,
    local_cot,
    valid,
    attend_scale,
    attend_offset,
    query_key_proj,
    heads_output_proj,
    heads_output_bias,
    feedforward_scale,
    feedforward_offset,
    feedforward_enlarge,
    feedforward_enlarge_bias,
    feedforward_contract,
    contract_bias,
):
    images, slots, width = arrived.shape
    heads_count = HEADS
    head_width = width // heads_count
    factor = 1.0 / math.sqrt(head_width)
    unrolled_entries = arrived.reshape(-1, width).astype(jnp.float32)
    valid_rows = valid.reshape(-1, 1)
    standardized_entries, scaled_prior_rows, inverse_prior_rms = norm_ahead_pass(
        unrolled_entries, attend_scale, attend_offset
    )
    normed_low = standardized_entries.astype(jnp.bfloat16)
    mixed_all = (
        product(normed_low, query_key_proj)
        .astype(jnp.bfloat16)
        .reshape(images, slots, 3, heads_count, head_width)
    )
    queries = mixed_all[:, :, 0]
    keys_all = mixed_all[:, :, 1]
    values_all = mixed_all[:, :, 2]
    raw_scores = (
        jnp.einsum("nqhe,nkhe->nhqk", queries, keys_all, preferred_element_type=jnp.float32)
        * factor
    )
    scores = jnp.where(valid[:, None, None, :] > 0.5, raw_scores, BLOCKED)
    peaks = jnp.max(scores, axis=-1, keepdims=True)
    powers = jnp.exp(scores - peaks)
    weights_soft = powers / jnp.sum(powers, axis=-1, keepdims=True)
    weights_low = weights_soft.astype(jnp.bfloat16)
    context = jnp.einsum(
        "nhqk,nkhe->nqhe", weights_low, values_all, preferred_element_type=jnp.float32
    )
    context = context.astype(jnp.bfloat16).reshape(-1, width)
    middle = unrolled_entries + product(context, heads_output_proj) + heads_output_bias
    hidden, scaled_mid, inverse_mid = norm_ahead_pass(middle, feedforward_scale, feedforward_offset)
    hidden_low = hidden.astype(jnp.bfloat16)
    widened = product(hidden_low, feedforward_enlarge) + feedforward_enlarge_bias
    activated = jax.nn.gelu(widened, approximate=False).astype(jnp.bfloat16)
    output = (middle + product(activated, feedforward_contract) + contract_bias) * valid_rows
    grad_out = local_cot.reshape(-1, width).astype(jnp.float32) * valid_rows
    grad_narrowshift = jnp.sum(grad_out, axis=0)
    out_low = grad_out.astype(jnp.bfloat16)
    grad_narrower = left_product(activated, out_low)
    grad_act = right_product(out_low, feedforward_contract)
    normal_cdf = 0.5 * (1.0 + lax.erf(widened * (1.0 / math.sqrt(2.0))))
    normal_pdf = jnp.exp(-0.5 * widened * widened) * (1.0 / math.sqrt(2.0 * math.pi))
    grad_wide = grad_act * (normal_cdf + widened * normal_pdf)
    grad_wideshift = jnp.sum(grad_wide, axis=0)
    wide_low = grad_wide.astype(jnp.bfloat16)
    grad_widener = left_product(hidden_low, wide_low)
    grad_mid_norm, grad_midgain, grad_midshift = norm_reverse_pass(
        right_product(wide_low, feedforward_enlarge), scaled_mid, inverse_mid, feedforward_scale
    )
    grad_middle = grad_out + grad_mid_norm
    grad_mixshift = jnp.sum(grad_middle, axis=0)
    middle_low = grad_middle.astype(jnp.bfloat16)
    grad_mixing = left_product(context, middle_low)
    grad_context = (
        right_product(middle_low, heads_output_proj)
        .astype(jnp.bfloat16)
        .reshape(images, slots, heads_count, head_width)
    )
    grad_values = jnp.einsum(
        "nhqk,nqhe->nkhe", weights_low, grad_context, preferred_element_type=jnp.float32
    )
    grad_weights = jnp.einsum(
        "nqhe,nkhe->nhqk", grad_context, values_all, preferred_element_type=jnp.float32
    )
    grad_scores = weights_soft * (
        grad_weights - jnp.sum(grad_weights * weights_soft, axis=-1, keepdims=True)
    )
    scores_low = grad_scores.astype(jnp.bfloat16)
    grad_queries = (
        jnp.einsum("nhqk,nkhe->nqhe", scores_low, keys_all, preferred_element_type=jnp.float32)
        * factor
    )
    grad_keys = (
        jnp.einsum("nhqk,nqhe->nkhe", scores_low, queries, preferred_element_type=jnp.float32)
        * factor
    )
    grad_mixed = (
        jnp.stack([grad_queries, grad_keys, grad_values], axis=2)
        .astype(jnp.bfloat16)
        .reshape(-1, 3 * width)
    )
    grad_attention = left_product(normed_low, grad_mixed)
    gradient_before_norm, gradient_prior_gain, gradient_prior_shift = norm_reverse_pass(
        right_product(grad_mixed, query_key_proj),
        scaled_prior_rows,
        inverse_prior_rms,
        attend_scale,
    )
    grad_hidden = (
        (grad_middle + gradient_before_norm).astype(jnp.bfloat16).reshape(images, slots, width)
    )
    output_full = output.reshape(images, slots, width)
    grads_two = (
        gradient_prior_gain,
        gradient_prior_shift,
        grad_attention,
        grad_mixing,
        grad_mixshift,
        grad_midgain,
        grad_midshift,
        grad_widener,
        grad_wideshift,
        grad_narrower,
        grad_narrowshift,
    )
    return (output_full.astype(jnp.bfloat16), grad_hidden, root_mean(output_full, valid), grads_two)


def block_skip(arrived, templates):
    images, slots, width = arrived.shape
    return (
        jnp.zeros((images, slots, width), jnp.bfloat16),
        jnp.zeros((images, slots, width), jnp.bfloat16),
        jnp.zeros((images,), jnp.float32),
        tuple((jnp.zeros(template.shape, jnp.float32) for template in templates)),
    )


def joint_sum(gradients):
    return lax.psum(gradients, ("section", "dp"))


def shards(
    entering_tokens,
    output_sensitivity,
    picture_tile_extents,
    pointwise_enlarge,
    enlarge_bias,
    channelwise_kernel,
    channelwise_conv_bias,
    pointwise_contract,
    convblock_scale,
    convblock_offset,
    attend_scale,
    attend_offset,
    query_key_proj,
    heads_output_proj,
    heads_output_bias,
    feedforward_scale,
    feedforward_offset,
    feedforward_enlarge,
    feedforward_enlarge_bias,
    feedforward_contract,
    contract_bias,
):
    micro_count = entering_tokens.shape[0]
    first = lax.axis_index("section") == 0
    templates_one = (
        pointwise_enlarge,
        enlarge_bias,
        channelwise_kernel,
        channelwise_conv_bias,
        pointwise_contract,
        convblock_scale,
        convblock_offset,
    )
    templates_two = (
        attend_scale,
        attend_offset,
        query_key_proj,
        heads_output_proj,
        heads_output_bias,
        feedforward_scale,
        feedforward_offset,
        feedforward_enlarge,
        feedforward_enlarge_bias,
        feedforward_contract,
        contract_bias,
    )
    sums_one = tuple((jnp.zeros(template.shape, jnp.float32) for template in templates_one))
    sums_two = tuple((jnp.zeros(template.shape, jnp.float32) for template in templates_two))
    ends_list = []
    means_list = []
    for micro_step in range(micro_count):
        valid = grid_mask(picture_tile_extents[micro_step])
        local_in = entering_tokens[micro_step]
        sent, kept = lax.cond(
            first,
            lambda: expand_forward(
                local_in,
                valid,
                pointwise_enlarge,
                enlarge_bias,
                channelwise_kernel,
                channelwise_conv_bias,
                pointwise_contract,
                convblock_scale,
                convblock_offset,
            ),
            lambda: expand_skip(local_in, pointwise_enlarge.shape[1]),
        )
        arrived = passed_along(sent, "section", 1)
        output, grad_hidden, rms_out, grads_two = lax.cond(
            first,
            lambda: block_skip(arrived, templates_two),
            lambda: block_pass(
                arrived,
                output_sensitivity[micro_step],
                valid,
                attend_scale,
                attend_offset,
                query_key_proj,
                heads_output_proj,
                heads_output_bias,
                feedforward_scale,
                feedforward_offset,
                feedforward_enlarge,
                feedforward_enlarge_bias,
                feedforward_contract,
                contract_bias,
            ),
        )
        returned = passed_along(grad_hidden, "section", -1)
        grad_inputs, rms_in, grads_one = lax.cond(
            first,
            lambda: expand_backward(
                local_in,
                valid,
                kept,
                returned,
                pointwise_enlarge,
                channelwise_kernel,
                pointwise_contract,
                convblock_scale,
            ),
            lambda: expand_back_skip(local_in, templates_one),
        )
        sums_one = jax.tree.map(lambda running, addend: running + addend, sums_one, grads_one)
        sums_two = jax.tree.map(lambda running, addend: running + addend, sums_two, grads_two)
        ends_list.append(jnp.where(first, grad_inputs, output))
        means_list.append(jnp.where(first, rms_in, rms_out))
    section_ends = jnp.stack(ends_list)[None]
    root_means = jnp.stack(means_list)[None]
    summed = joint_sum(sums_one + sums_two)
    return (section_ends, root_means) + tuple(summed)


def solution(mesh):
    placed = (
        P(None, "dp", None, None),
        P(None, "dp", None, None),
        P(None, "dp", None),
        P(),
        P(),
        P(),
        P(),
        P(),
        P(),
        P(),
        P(),
        P(),
        P(),
        P(),
        P(),
        P(),
        P(),
        P(),
        P(),
        P(),
        P(),
    )
    return jax.shard_map(
        shards,
        mesh=mesh,
        in_specs=placed,
        out_specs=(
            P("section", None, "dp", None, None),
            P("section", None, "dp"),
            P(),
            P(),
            P(),
            P(),
            P(),
            P(),
            P(),
            P(),
            P(),
            P(),
            P(),
            P(),
            P(),
            P(),
            P(),
            P(),
            P(),
            P(),
        ),
        check_vma=False,
    )
```

profile of v0, /device:TPU:1, one launch (start us, length us, event | category | flops | bytes accessed | tf_op | source)
XLA Modules:
  0.0 709.3 jit_solution(13336461958036388458)
XLA Ops:
  12.5 11.4 %conditional.21 = (bf16[1,256,384]{2,1,0:T(8,128)(2,1)}, f32[1,18,18,1536]{3,2,1,0:T(8,128)}, f32[1,16,16,1536]{3,2,1,0:T(8,128)}, bf16[256,1536]{1,0:T(8,128)(2...) conditional(s32[]{:T(128)} %convert_element_type.551, () %tuple.123, ...), branch_computations={%region_135.136_spmd, %region_136.139_spmd} | conditional | flops 614891776 | bytes 20864092 | solution.py:382
  16.0 3.2 multiply_convert_fusion.7
  28.0 11.2 %conditional.15 = (bf16[1,256,384]{2,1,0:T(8,128)(2,1)}, f32[1,18,18,1536]{3,2,1,0:T(8,128)}, f32[1,16,16,1536]{3,2,1,0:T(8,128)}, bf16[256,1536]{1,0:T(8,128)(2...) conditional(s32[]{:T(128)} %convert_element_type.551, () %tuple.111, (bf16[1,1,256,384]{3,2,1,0:T(8,128)(2,1)S(1)}, ...), branch_computations={%region_45.46_spmd, %region_46.49_spmd} | conditional | flops 614891776 | bytes 20864092 | solution.py:382
  43.2 12.6 %conditional.12 = (bf16[1,256,384]{2,1,0:T(8,128)(2,1)}, f32[1,18,18,1536]{3,2,1,0:T(8,128)}, f32[1,16,16,1536]{3,2,1,0:T(8,128)}, bf16[256,1536]{1,0:T(8,128)(2...) conditional(s32[]{:T(128)} %convert_element_type.551, () %tuple.105, (bf16[1,1,256,384]{3,2,1,0:T(8,128)(2,1)S(1)}, ...), branch_computations={%region_0.0_spmd, %region_1.4_spmd} | conditional | flops 614891776 | bytes 17718336 | solution.py:382
  46.7 3.3 multiply_convert_fusion.4
  59.9 13.8 %conditional.18 = (bf16[1,256,384]{2,1,0:T(8,128)(2,1)S(1)}, f32[1,18,18,1536]{3,2,1,0:T(8,128)}, f32[1,16,16,1536]{3,2,1,0:T(8,128)}, bf16[256,1536]{1,0:T(8,12...) conditional(s32[]{:T(128)} %convert_element_type.551, () %tuple.117, ...), branch_computations={%region_90.91_spmd, %region_91.94_spmd} | conditional | flops 614891776 | bytes 18510968 | solution.py:382
  64.5 3.3 multiply_convert_fusion.6
  75.8 5.0 conditional.13
  83.7 6.5 conditional.16
  93.1 6.1 conditional.22
  102.2 5.1 conditional.19
  109.6 5.1 add_add_fusion
  125.2 37.8 %conditional.14 = (bf16[1,256,384]{2,1,0:T(8,128)(2,1)S(1)}, f32[1]{0:T(128)}, f32[1536]{0:T(1024)S(1)}, f32[9,1536]{1,0:T(8,128)S(1)}, f32[1536]{0:T(1024)S(1)}...) conditional(s32[]{:T(128)} %convert_element_type.551, () %tuple.104, ...), branch_computations={%region_26.27_spmd, %region_27.45_spmd} | conditional | flops 1229274112 | bytes 44717720 | solution.py:419
  129.8 10.2 %multiply_reduce_fusion.29 = (f32[1536]{0:T(1024)S(1)}, f32[1536]{0:T(1024)S(1)}, f32[1536]{0:T(1024)S(1)}, f32[1536]{0:T(1024)S(1)}, f32[1536]{0:T(1024)S(1)}, ...) fusion(f32[1,18,18,1536]{3,2,1,0:T(8,128)} %get-tuple-element.3, ...), kind=kOutput, calls=%fused_computation.527 | convolution fusion | flops 313279488 | bytes 19137024 | tf_op jit(solution)/shard_map/cond/branch_1_fun/na,ba->nb/dot_general | solution.py:56
  140.5 6.8 fusion.428
  150.4 3.3 convolution_bitcast_fusion.4
  163.8 52.9 %conditional.17 = (bf16[1,256,384]{2,1,0:T(8,128)(2,1)}, f32[1]{0:T(128)}, f32[1536]{0:T(1024)}, f32[9,1536]{1,0:T(8,128)}, f32[1536]{0:T(1024)}, /*index=5*/f32...) conditional(s32[]{:T(128)} %convert_element_type.551, () %tuple.110, ...), branch_computations={%region_71.72_spmd, %region_72.90_spmd} | conditional | flops 1229274112 | bytes 44754808 | solution.py:419
  170.1 12.2 %multiply_reduce_fusion.40 = (f32[1536]{0:T(1024)S(1)}, f32[1536]{0:T(1024)S(1)}, f32[1536]{0:T(1024)S(1)}, f32[1536]{0:T(1024)S(1)}, f32[1536]{0:T(1024)S(1)}, ...) fusion(f32[1,18,18,1536]{3,2,1,0:T(8,128)} %get-tuple-element.3, ...), kind=kOutput, calls=%fused_computation.611 | convolution fusion | flops 313279488 | bytes 19137024 | tf_op jit(solution)/shard_map/cond/branch_1_fun/na,ba->nb/dot_general | solution.py:56
  192.6 7.4 %fusion.430 = (f32[1536]{0:T(1024)}, bf16[1,16,16,1536]{3,2,1,0:T(8,128)(2,1)S(1)}) fusion(f32[16,16]{1,0:T(8,128)S(1)} %mul.1769, f32[1536]{0:T(1024)S(1)} %get-tuple-element.824, f32[1536]{0:T(1024)S(1)} %get-tuple-element.825, f32[1536]{0:T(1024)S(1)} %get-tuple-element.826, f32[1536]{0:T(1024)S(1)} %get-tuple-element.827, ...), kind=kLoop, calls=%fused_computation.865 | loop fusion | flops 7862784 | bytes 2421760 | tf_op jit(solution)/shard_map/cond/branch_1_fun/reduce_sum | solution.py:161
  203.9 3.4 convolution_bitcast_fusion.6
  210.4 3.2 convolution_bitcast_fusion.7
  217.3 50.5 %conditional.23 = (bf16[1,256,384]{2,1,0:T(8,128)(2,1)}, f32[1]{0:T(128)}, f32[1536]{0:T(1024)S(1)}, f32[9,1536]{1,0:T(8,128)}, f32[1536]{0:T(1024)S(1)}, /*inde...) conditional(s32[]{:T(128)} %convert_element_type.551, () %tuple.122, ...), branch_computations={%region_161.162_spmd, %region_162.180_spmd} | conditional | flops 1229274112 | bytes 48727984 | solution.py:419
  223.0 12.0 %multiply_reduce_fusion.62 = (f32[1536]{0:T(1024)S(1)}, f32[1536]{0:T(1024)S(1)}, f32[1536]{0:T(1024)S(1)}, f32[1536]{0:T(1024)S(1)}, f32[1536]{0:T(1024)S(1)}, ...) fusion(f32[1,18,18,1536]{3,2,1,0:T(8,128)} %get-tuple-element.4, ...), kind=kOutput, calls=%fused_computation.779 | convolution fusion | flops 313279488 | bytes 19137024 | tf_op jit(solution)/shard_map/cond/branch_1_fun/na,ba->nb/dot_general | solution.py:56
  245.4 7.4 %fusion.434 = (f32[1536]{0:T(1024)}, bf16[1,16,16,1536]{3,2,1,0:T(8,128)(2,1)S(1)}) fusion(f32[16,16]{1,0:T(8,128)S(1)} %mul.2055, f32[1536]{0:T(1024)S(1)} %get-tuple-element.890, f32[1536]{0:T(1024)S(1)} %get-tuple-element.891, f32[1536]{0:T(1024)S(1)} %get-tuple-element.892, f32[1536]{0:T(1024)S(1)} %get-tuple-element.893, ...), kind=kLoop, calls=%fused_computation.867 | loop fusion | flops 7862784 | bytes 2421760 | tf_op jit(solution)/shard_map/cond/branch_1_fun/reduce_sum | solution.py:161
  268.4 37.8 %conditional.20 = (bf16[1,256,384]{2,1,0:T(8,128)(2,1)}, f32[1]{0:T(128)}, f32[1536]{0:T(1024)}, f32[9,1536]{1,0:T(8,128)}, f32[1536]{0:T(1024)S(1)}, /*index=5*...) conditional(s32[]{:T(128)} %convert_element_type.551, () %tuple.116, ...), branch_computations={%region_116.117_spmd, %region_117.135_spmd} | conditional | flops 1229274112 | bytes 44164900 | solution.py:419
  275.1 11.0 %multiply_reduce_fusion.51 = (f32[1536]{0:T(1024)S(1)}, f32[1536]{0:T(1024)S(1)}, f32[1536]{0:T(1024)S(1)}, f32[1536]{0:T(1024)S(1)}, f32[1536]{0:T(1024)S(1)}, ...) fusion(f32[1,18,18,1536]{3,2,1,0:T(8,128)} %get-tuple-element.3, ...), kind=kOutput, calls=%fused_computation.695 | convolution fusion | flops 313279488 | bytes 19137024 | tf_op jit(solution)/shard_map/cond/branch_1_fun/na,ba->nb/dot_general | solution.py:56
  287.8 8.4 %fusion.432 = (f32[1536]{0:T(1024)}, bf16[1,16,16,1536]{3,2,1,0:T(8,128)(2,1)S(1)}) fusion(f32[16,16]{1,0:T(8,128)S(1)} %mul.1912, f32[1536]{0:T(1024)S(1)} %get-tuple-element.857, f32[1536]{0:T(1024)S(1)} %get-tuple-element.858, f32[1536]{0:T(1024)S(1)} %get-tuple-element.859, f32[1536]{0:T(1024)S(1)} %get-tuple-element.860, ...), kind=kLoop, calls=%fused_computation.866 | loop fusion | flops 7862784 | bytes 2421760 | tf_op jit(solution)/shard_map/cond/branch_1_fun/reduce_sum | solution.py:161
  306.3 5.7 add_add_fusion.2
  316.3 6.2 add_add_fusion.3
  326.6 120.0 %all-reduce.13.cloned.1.call-done = (f32[1536]{0:T(1024)}, f32[9,1536]{1,0:T(8,128)}, f32[1536]{0:T(1024)}, f32[384]{0:T(512)}, f32[384]{0:T(512)}, /*index=5*/f...) async-done(((f32[1536]{0:T(1024)}, f32[9,1536]{1,0:T(8,128)}, f32[1536]{0:T(1024)}, ...) | async-done | bytes 86032 | tf_op jit(solution)/shard_map/psum | solution.py:325
  446.6 238.2 %all-reduce.15.cloned.1.call-done = (f32[384,1536]{1,0:T(8,128)}, f32[1536,384]{1,0:T(8,128)}, f32[384,1152]{1,0:T(8,128)}, f32[384,384]{1,0:T(8,128)}, f32[384,1536]{1,0:T(8,128)}, /*index=5*/f32[1536,384]{1,0:T(8,128)}) async-done(((f32[384,1536]{1,0:T(8,128)}, f32[1536,384]{1,0:T(8,128)}, f32[384,1152]{1,0:T(8,128)}, f32[384,384]{1,0:T(8,128)}, f32[384,1536]{1,0:T(8,128)}, ...) | async-done | bytes 11796496 | tf_op jit(solution)/shard_map/psum | solution.py:325
  684.8 3.4 copy.425
  (613 shorter events, 209.7 us)
Async XLA Ops:
  7.3 439.4 %all-reduce.13.cloned.1.call-start = ((), (), s32[]{:S(2)}) async-start(), calls=%async_computation | async-start | bytes 278528 | tf_op jit(solution)/shard_map/psum | solution.py:325
  11.8 15.6 %copy-start.41 = (bf16[1,1,256,384]{3,2,1,0:T(8,128)(2,1)}, bf16[1,1,256,384]{3,2,1,0:T(8,128)(2,1)S(1)}, u32[]{:S(2)}) copy-start(bf16[1,1,256,384]{3,2,1,0:T(8,128)(2,1)S(1)} %get-tuple-element.1051) | copy-start | bytes 589828
  11.8 30.8 %copy-start.42 = (bf16[1,1,256,384]{3,2,1,0:T(8,128)(2,1)}, bf16[1,1,256,384]{3,2,1,0:T(8,128)(2,1)S(1)}, u32[]{:S(2)}) copy-start(bf16[1,1,256,384]{3,2,1,0:T(8,128)(2,1)S(1)} %get-tuple-element.1050) | copy-start | bytes 589828
  11.9 48.1 %copy-start.37 = (bf16[1,1,256,384]{3,2,1,0:T(8,128)(2,1)}, bf16[1,1,256,384]{3,2,1,0:T(8,128)(2,1)S(1)}, u32[]{:S(2)}) copy-start(bf16[1,1,256,384]{3,2,1,0:T(8,128)(2,1)S(1)} %get-tuple-element.1053) | copy-start | bytes 589828
  23.9 67.7 %collective-permute-start.6 = (bf16[1,256,384]{2,1,0:T(8,128)(2,1)}, bf16[1,256,384]{2,1,0:T(8,128)(2,1)S(1)}, u32[]{:S(2)}, u32[]{:S(2)}) collective-permute-start(bf16[1,256,384]{2,1,0:T(8,128)(2,1)} %get-tuple-element.583), channel_id=1, source_target_pairs={{0,16},{1,17},{2,18},{3,19},{4,20},{5,21},{6,22},{7,23},{8,24},{9,... | collective-permute-start | bytes 589832 | tf_op jit(solution)/shard_map/ppermute | solution.py:19
  39.2 43.0 %collective-permute-start.2 = (bf16[1,256,384]{2,1,0:T(8,128)(2,1)}, bf16[1,256,384]{2,1,0:T(8,128)(2,1)S(1)}, u32[]{:S(2)}, u32[]{:S(2)}) collective-permute-start(bf16[1,256,384]{2,1,0:T(8,128)(2,1)} %get-tuple-element.565), channel_id=1, source_target_pairs={{0,16},{1,17},{2,18},{3,19},{4,20},{5,21},{6,22},{7,23},{8,24},{9,... | collective-permute-start | bytes 589832 | tf_op jit(solution)/shard_map/ppermute | solution.py:19
  55.9 19.9 %collective-permute-start = (bf16[1,256,384]{2,1,0:T(8,128)(2,1)}, bf16[1,256,384]{2,1,0:T(8,128)(2,1)S(1)}, u32[]{:S(2)}, u32[]{:S(2)}) collective-permute-start(bf16[1,256,384]{2,1,0:T(8,128)(2,1)} %get-tuple-element.556), channel_id=1, source_target_pairs={{0,16},{1,17},{2,18},{3,19},{4,20},{5,21},{6,22},{7,23},{8,24},{9,... | collective-permute-start | bytes 589832 | tf_op jit(solution)/shard_map/ppermute | solution.py:19
  59.9 15.8 %copy-start = (bf16[384,384]{1,0:T(8,128)(2,1)S(1)}, bf16[384,384]{1,0:T(8,128)(2,1)}, u32[]{:S(2)}) copy-start(bf16[384,384]{1,0:T(8,128)(2,1)} %param.58) | copy-start | bytes 884740
  59.9 15.8 %copy-start.3 = (bf16[384,1152]{1,0:T(8,128)(2,1)S(1)}, bf16[384,1152]{1,0:T(8,128)(2,1)}, u32[]{:S(2)}) copy-start(bf16[384,1152]{1,0:T(8,128)(2,1)} %param.57) | copy-start | bytes 2654212
  59.9 15.8 %copy-start.103 = (f32[384]{0:T(512)S(1)}, f32[384]{0:T(512)}, u32[]{:S(2)}) copy-start(f32[384]{0:T(512)} %param.55) | copy-start | bytes 4612
  74.4 26.2 %collective-permute-start.4 = (bf16[1,256,384]{2,1,0:T(8,128)(2,1)}, bf16[1,256,384]{2,1,0:T(8,128)(2,1)S(1)}, u32[]{:S(2)}, u32[]{:S(2)}) collective-permute-start(bf16[1,256,384]{2,1,0:T(8,128)(2,1)} %copy-done.108), channel_id=1, source_target_pairs={{0,16},{1,17},{2,18},{3,19},{4,20},{5,21},{6,22},{7,23},{8,24},{9,... | collective-permute-start | bytes 589832 | tf_op jit(solution)/shard_map/ppermute | solution.py:19
  80.9 44.3 %collective-permute-start.1 = (bf16[1,256,384]{2,1,0:T(8,128)(2,1)}, bf16[1,256,384]{2,1,0:T(8,128)(2,1)}, u32[]{:S(2)}, u32[]{:S(2)}) collective-permute-start(bf16[1,256,384]{2,1,0:T(8,128)(2,1)} %get-tuple-element.557), channel_id=1, source_target_pairs={{16,0},{17,1},{18,2},{19,3},{20,4},{21,5},{22,6},{23,7},{24,8},{25... | collective-permute-start | bytes 589832 | tf_op jit(solution)/shard_map/ppermute | solution.py:19
  90.3 72.8 %collective-permute-start.3 = (bf16[1,256,384]{2,1,0:T(8,128)(2,1)}, bf16[1,256,384]{2,1,0:T(8,128)(2,1)}, u32[]{:S(2)}, u32[]{:S(2)}) collective-permute-start(bf16[1,256,384]{2,1,0:T(8,128)(2,1)} %get-tuple-element.566), channel_id=1, source_target_pairs={{16,0},{17,1},{18,2},{19,3},{20,4},{21,5},{22,6},{23,7},{24,8},{25... | collective-permute-start | bytes 589832 | tf_op jit(solution)/shard_map/ppermute | solution.py:19
  99.4 117.4 %collective-permute-start.7 = (bf16[1,256,384]{2,1,0:T(8,128)(2,1)}, bf16[1,256,384]{2,1,0:T(8,128)(2,1)}, u32[]{:S(2)}, u32[]{:S(2)}) collective-permute-start(bf16[1,256,384]{2,1,0:T(8,128)(2,1)} %get-tuple-element.584), channel_id=1, source_target_pairs={{16,0},{17,1},{18,2},{19,3},{20,4},{21,5},{22,6},{23,7},{24,8},{25... | collective-permute-start | bytes 589832 | tf_op jit(solution)/shard_map/ppermute | solution.py:19
  107.4 160.5 %collective-permute-start.5 = (bf16[1,256,384]{2,1,0:T(8,128)(2,1)}, bf16[1,256,384]{2,1,0:T(8,128)(2,1)}, u32[]{:S(2)}, u32[]{:S(2)}) collective-permute-start(bf16[1,256,384]{2,1,0:T(8,128)(2,1)} %get-tuple-element.575), channel_id=1, source_target_pairs={{16,0},{17,1},{18,2},{19,3},{20,4},{21,5},{22,6},{23,7},{24,8},{25... | collective-permute-start | bytes 589832 | tf_op jit(solution)/shard_map/ppermute | solution.py:19
  125.2 38.6 %copy-start.164 = (f32[1,256]{1,0:T(1,128)S(1)}, f32[1,256]{1,0:T(1,128)}, u32[]{:S(2)}) copy-start(f32[1,256]{1,0:T(1,128)} %copy-done.163) | copy-start | bytes 3076
  163.8 53.0 %copy-start.16 = (bf16[256,1536]{1,0:T(8,128)(2,1)S(1)}, bf16[256,1536]{1,0:T(8,128)(2,1)}, u32[]{:S(2)}) copy-start(bf16[256,1536]{1,0:T(8,128)(2,1)} %get-tuple-element.589) | copy-start | bytes 2359300
  163.8 53.0 %copy-start.27 = (f32[256,384]{1,0:T(8,128)S(1)}, f32[256,384]{1,0:T(8,128)}, u32[]{:S(2)}) copy-start(f32[256,384]{1,0:T(8,128)} %copy-done.26) | copy-start | bytes 1179652
  163.8 53.0 %copy-start.157 = (f32[1,256]{1,0:T(1,128)S(1)}, f32[1,256]{1,0:T(1,128)}, u32[]{:S(2)}) copy-start(f32[1,256]{1,0:T(1,128)} %copy-done.156) | copy-start | bytes 3076
  164.2 18.1 %copy-start.167 = (f32[1,256]{1,0:T(1,128)}, f32[1,256]{1,0:T(1,128)S(1)}, u32[]{:S(2)}) copy-start(f32[1,256]{1,0:T(1,128)S(1)} %get-tuple-element.345) | copy-start | bytes 3076 | tf_op jit(solution)/shard_map/cond
  170.1 12.2 %copy-start.220 = (f32[256]{0:T(256)}, f32[256]{0:T(256)S(1)}, u32[]{:S(2)}) copy-start(f32[256]{0:T(256)S(1)} %get-tuple-element.1040) | copy-start | bytes 3076 | tf_op jit(solution)/shard_map/cond
  170.1 12.2 %copy-start.222 = (f32[256]{0:T(256)}, f32[256]{0:T(256)S(1)}, u32[]{:S(2)}) copy-start(f32[256]{0:T(256)S(1)} %get-tuple-element.1041) | copy-start | bytes 3076 | tf_op jit(solution)/shard_map/cond
  191.2 8.8 %copy-start.168 = (f32[1,256]{1,0:T(1,128)S(1)}, f32[1,256]{1,0:T(1,128)}, u32[]{:S(2)}) copy-start(f32[1,256]{1,0:T(1,128)} %copy-done.167) | copy-start | bytes 3076 | tf_op jit(solution)/shard_map/cond
  223.0 12.0 %copy-start.224 = (f32[256]{0:T(256)}, f32[256]{0:T(256)S(1)}, u32[]{:S(2)}) copy-start(f32[256]{0:T(256)S(1)} %get-tuple-element.1048) | copy-start | bytes 3076 | tf_op jit(solution)/shard_map/cond
  223.0 12.0 %copy-start.226 = (f32[256]{0:T(256)}, f32[256]{0:T(256)S(1)}, u32[]{:S(2)}) copy-start(f32[256]{0:T(256)S(1)} %get-tuple-element.1049) | copy-start | bytes 3076 | tf_op jit(solution)/shard_map/cond
  275.1 11.1 %copy-start.228 = (f32[256]{0:T(256)}, f32[256]{0:T(256)S(1)}, u32[]{:S(2)}) copy-start(f32[256]{0:T(256)S(1)} %get-tuple-element.1044) | copy-start | bytes 3076 | tf_op jit(solution)/shard_map/cond
  275.1 11.1 %copy-start.229 = (f32[256]{0:T(256)}, f32[256]{0:T(256)S(1)}, u32[]{:S(2)}) copy-start(f32[256]{0:T(256)S(1)} %get-tuple-element.1045) | copy-start | bytes 3076 | tf_op jit(solution)/shard_map/cond
  275.1 12.6 %copy-start.61 = (f32[9,1536]{1,0:T(8,128)S(1)}, f32[9,1536]{1,0:T(8,128)}, u32[]{:S(2)}) copy-start(f32[9,1536]{1,0:T(8,128)} %get-tuple-element.379) | copy-start | bytes 165892 | tf_op jit(solution)/shard_map/cond
  286.1 10.1 %copy-start.162 = (f32[1,256]{1,0:T(1,128)S(1)}, f32[1,256]{1,0:T(1,128)}, u32[]{:S(2)}) copy-start(f32[1,256]{1,0:T(1,128)} %get-tuple-element.380) | copy-start | bytes 3076 | tf_op jit(solution)/shard_map/cond
  306.2 8.7 %copy-start.139 = (f32[1536]{0:T(1024)S(1)}, f32[1536]{0:T(1024)}, u32[]{:S(2)}) copy-start(f32[1536]{0:T(1024)} %copy-done.138) | copy-start | bytes 18436
  306.2 8.7 %copy-start.141 = (f32[1536]{0:T(1024)S(1)}, f32[1536]{0:T(1024)}, u32[]{:S(2)}) copy-start(f32[1536]{0:T(1024)} %copy-done.140) | copy-start | bytes 18436
  316.3 368.5 %all-reduce.15.cloned.1.call-start = ((), (), s32[]{:S(2)}) async-start(), calls=%async_computation.1 | async-start | bytes 23592960 | tf_op jit(solution)/shard_map/psum | solution.py:325
  (149 other events, 451.3 us)
Sparse Core Ops, SparseCore 0:
  316.4 130.1 all-reduce.12
  455.3 229.4 all-reduce.14
where the time goes:
time: 722 us; the launch traced here: 709 us
  waiting for transfers between devices  358 us (50%)
  local copies, waits for them, and re-layouts  113 us (16%)
  other arithmetic  112 us (16%)
  matrix products  89.6 us (12%)
  between operations  15.8 us (2%)
  starting transfers between devices  10.4 us (1%)
  loops' own time  10.3 us (1%)
    psum x2, waiting for transfers between devices, joint_sum(): return lax.psum(gradients, ('section', 'dp'))  358 us
    dot_general x8, matrix products, right_product(): jnp.einsum('na,ba->nb', left, right, preferred_element_type=jnp.float32)  56.8 us
    unnamed x298, local copies, waits for them, and re-layouts  30.4 us
    reduce_sum x4, other arithmetic, expand_backward(): grad_upshift = jnp.sum(grad_expanded, axis=0)  30 us
    add x13, other arithmetic, shards(): running + addend  28.6 us
    another operation x60, local copies, waits for them, and re-layouts  23.6 us
    cond x8, local copies, waits for them, and re-layouts, shards(): lax.cond(first, lambda: expand_backward(local_in, valid, kept, returned,...  22.6 us
    dot_general x8, matrix products, left_product(): jnp.einsum('na,nb->ab', left, right, preferred_element_type=jnp.float32)  20.5 us
  transfers between devices with their start and end apart: 10, of which 2 were waited for; matrix products, arithmetic and copies ran while one was open for 31% of the time, Pallas kernels for 0%

commit v1 on v0

v1 whole, which is shorter than its diff:
```python
import functools
import math

import jax
import jax.numpy as jnp
from jax import lax
from jax.experimental import pallas as pl
from jax.experimental.pallas import tpu as pltpu
from jax.sharding import PartitionSpec as P

HEADS = 6
SIDE = 16
SLOTS = SIDE * SIDE
EPSILON = 1e-05
BLOCKED = -1000000000.0
LANES = 128
BLOCK = 256
BF16 = jnp.bfloat16
F32 = jnp.float32


def dot_nn(left, right):
    return jnp.dot(left, right, preferred_element_type=F32)


def dot_nt(left, right):
    return lax.dot_general(left, right, (((1,), (1,)), ((), ())), preferred_element_type=F32)


def dot_tn(left, right):
    return lax.dot_general(left, right, (((0,), (0,)), ((), ())), preferred_element_type=F32)


def norm_parts(values):
    centered = values - jnp.mean(values, axis=-1, keepdims=True)
    inverse = lax.rsqrt(jnp.mean(centered * centered, axis=-1, keepdims=True) + EPSILON)
    return centered * inverse, inverse


def norm_reverse(upstream, scaled, inverse, gain):
    lifted = upstream * gain
    return inverse * (
        lifted
        - jnp.mean(lifted, axis=-1, keepdims=True)
        - scaled * jnp.mean(lifted * scaled, axis=-1, keepdims=True)
    )


def total_rows(values):
    return jnp.sum(values, axis=0, keepdims=True)


def valid_column(numbers, image):
    slot = lax.broadcasted_iota(jnp.int32, (SLOTS, 1), 0)
    inside = (slot // SIDE < numbers[1 + 2 * image]) & (slot % SIDE < numbers[2 + 2 * image])
    return inside.astype(F32)


def valid_rows(numbers, images):
    return jnp.concatenate([valid_column(numbers, image) for image in range(images)], axis=0)


def column_shifts(row, first_column, last_column):
    before = jnp.where(first_column, 0.0, pltpu.roll(row, 1, 0))
    after = jnp.where(last_column, 0.0, pltpu.roll(row, SIDE - 1, 0))
    return before, after


def conv_ahead_kernel(
    numbers, tokens, enlarge, enlarge_bias, taps, taps_bias, contract, gain, shift,
    sent, expanded, slope, active, projected, grid_cells,
):
    rows = sent.shape[0]
    images = rows // SLOTS
    width = sent.shape[1]
    channels = enlarge.shape[1]
    local_in = tokens[...].reshape(rows, width)
    valid = valid_rows(numbers, images)
    column = lax.broadcasted_iota(jnp.int32, (SIDE, BLOCK), 0)
    first_column, last_column = column == 0, column == SIDE - 1
    total = jnp.zeros((rows, width), F32)
    for start in range(0, channels, BLOCK):
        part = slice(start, start + BLOCK)
        cells = (dot_nn(local_in, enlarge[:, part]) + enlarge_bias[:, part]) * valid
        grid_cells[...] = cells
        expanded[:, part] = cells.astype(BF16)
        kernel = [taps[tap : tap + 1, part] for tap in range(9)]
        bias = taps_bias[:, part]
        for image in range(images):
            base = image * SLOTS
            above = here = None
            for line in range(SIDE + 1):
                if line < SIDE:
                    row = grid_cells[base + line * SIDE : base + (line + 1) * SIDE, :]
                    before, after = column_shifts(row, first_column, last_column)
                    sums = [
                        before * kernel[3 * a] + row * kernel[3 * a + 1] + after * kernel[3 * a + 2]
                        for a in range(3)
                    ]
                if line > 0:
                    convolved = above + sums[2] if line < SIDE else above
                    gate = jax.nn.sigmoid(convolved)
                    lit = convolved * gate
                    place = slice(base + (line - 1) * SIDE, base + line * SIDE)
                    active[place, part] = lit.astype(BF16)
                    slope[place, part] = (gate + lit * (1.0 - gate)).astype(BF16)
                if line < SIDE:
                    above = (here if line > 0 else bias) + sums[1]
                    here = bias + sums[0]
        total = total + dot_nn(active[:, part], contract[part, :])
    projected[...] = total
    scaled, _ = norm_parts(total)
    sent[...] = (local_in.astype(F32) + scaled * gain[...] + shift[...]).astype(BF16)


def head_lanes(width):
    return lax.broadcasted_iota(jnp.int32, (1, width), 1)


def attend_ahead_kernel(
    numbers, sent, gain, shift, mixing_in, mixing_out, mixing_bias,
    qkv, weights, context, middle,
):
    rows, width = sent.shape
    images = rows // SLOTS
    head = width // HEADS
    factor = 1.0 / math.sqrt(head)
    entering = sent[...].astype(F32)
    scaled, _ = norm_parts(entering)
    normed = (scaled * gain[...] + shift[...]).astype(BF16)
    for start in range(0, 3 * width, width):
        part = slice(start, start + width)
        qkv[:, part] = dot_nn(normed, mixing_in[:, part]).astype(BF16)
    pair = 2 * head
    lane = head_lanes(pair)
    for image in range(images):
        valid = valid_column(numbers, image) > 0.5
        place = slice(image * SLOTS, (image + 1) * SLOTS)
        for couple in range(HEADS // 2):
            at = couple * pair
            queries = qkv[place, at : at + pair]
            keys = qkv[place, width + at : width + at + pair]
            values = qkv[place, 2 * width + at : 2 * width + at + pair]
            gathered = []
            for side in range(2):
                own = (lane >= side * head) & (lane < (side + 1) * head)
                scores = dot_nt(jnp.where(own, keys, jnp.zeros_like(keys)), queries) * factor
                scores = jnp.where(valid, scores, BLOCKED)
                powers = jnp.exp(scores - jnp.max(scores, axis=0, keepdims=True))
                soft = powers * (1.0 / jnp.sum(powers, axis=0, keepdims=True))
                low = soft.astype(BF16)
                weights[image * HEADS + couple * 2 + side] = low
                gathered.append(dot_tn(low, values))
            context[place, at : at + pair] = jnp.where(lane < head, *gathered).astype(BF16)
    middle[...] = entering + dot_nn(context[...], mixing_out[...]) + mixing_bias[...]


def mlp_kernel(
    numbers, middle, sensitivity, gain, shift, enlarge, enlarge_bias, contract, contract_bias,
    output, grad_middle, narrower, widener, small, wide_small,
):
    rows, width = middle.shape
    images = rows // SLOTS
    hidden_width = enlarge.shape[1]
    valid = valid_rows(numbers, images)
    center = middle[...]
    scaled, inverse = norm_parts(center)
    hidden = (scaled * gain[...] + shift[...]).astype(BF16)
    grad_out = sensitivity[...].reshape(rows, width).astype(F32) * valid
    out_low = grad_out.astype(BF16)
    total = jnp.zeros((rows, width), F32)
    grad_hidden = jnp.zeros((rows, width), F32)
    for start in range(0, hidden_width, BLOCK):
        part = slice(start, start + BLOCK)
        widened = dot_nn(hidden, enlarge[:, part]) + enlarge_bias[:, part]
        normal_cdf = 0.5 * (1.0 + lax.erf(widened * (1.0 / math.sqrt(2.0))))
        normal_pdf = jnp.exp(-0.5 * widened * widened) * (1.0 / math.sqrt(2.0 * math.pi))
        activated = (widened * normal_cdf).astype(BF16)
        total = total + dot_nn(activated, contract[part, :])
        grad_wide = dot_nt(out_low, contract[part, :]) * (normal_cdf + widened * normal_pdf)
        wide_small[:, part] = total_rows(grad_wide)
        wide_low = grad_wide.astype(BF16)
        grad = dot_tn(activated, out_low).astype(BF16)
        for lanes in range(width // LANES):
            narrower[lanes, part, :] = grad[:, lanes * LANES : (lanes + 1) * LANES]
        grad = dot_tn(hidden, wide_low).astype(BF16)
        for lanes in range(BLOCK // LANES):
            widener[start // LANES + lanes] = grad[:, lanes * LANES : (lanes + 1) * LANES]
        grad_hidden = grad_hidden + dot_nt(wide_low, enlarge[:, part])
    output[...] = ((center + total + contract_bias[...]) * valid).astype(BF16)
    gradient = grad_out + norm_reverse(grad_hidden, scaled, inverse, gain[...])
    grad_middle[...] = gradient
    small[0:1, :] = total_rows(grad_out)
    small[1:2, :] = total_rows(grad_hidden * scaled)
    small[2:3, :] = total_rows(grad_hidden)
    small[3:4, :] = total_rows(gradient)


def attend_back_kernel(
    sent, grad_middle, qkv, weights, context, gain, shift, mixing_in, mixing_out,
    grad_sent, mixed, small, grad_qkv,
):
    rows, width = sent.shape
    images = rows // SLOTS
    head = width // HEADS
    factor = 1.0 / math.sqrt(head)
    gradient = grad_middle[...]
    middle_low = gradient.astype(BF16)
    blocks = width // LANES
    grad = dot_tn(context[...], middle_low).astype(BF16)
    for lanes in range(blocks):
        mixed[3 * blocks + lanes] = grad[:, lanes * LANES : (lanes + 1) * LANES]
    grad_context = dot_nt(middle_low, mixing_out[...]).astype(BF16)
    pair = 2 * head
    lane = head_lanes(pair)
    for image in range(images):
        place = slice(image * SLOTS, (image + 1) * SLOTS)
        for couple in range(HEADS // 2):
            at = couple * pair
            queries = qkv[place, at : at + pair]
            keys = qkv[place, width + at : width + at + pair]
            values = qkv[place, 2 * width + at : 2 * width + at + pair]
            upstream = grad_context[place, at : at + pair]
            parts = []
            for side in range(2):
                own = (lane >= side * head) & (lane < (side + 1) * head)
                low = weights[image * HEADS + couple * 2 + side]
                soft = low.astype(F32)
                grad_values = dot_nn(low, upstream)
                lifted = soft * dot_nt(jnp.where(own, values, jnp.zeros_like(values)), upstream)
                scores_low = (lifted - soft * jnp.sum(lifted, axis=0, keepdims=True)).astype(BF16)
                parts.append(
                    (
                        dot_tn(scores_low, keys) * factor,
                        dot_nn(scores_low, queries) * factor,
                        grad_values,
                    )
                )
            for which in range(3):
                merged = jnp.where(lane < head, parts[0][which], parts[1][which])
                grad_qkv[place, which * width + at : which * width + at + pair] = merged.astype(
                    BF16
                )
    entering = sent[...].astype(F32)
    scaled, inverse = norm_parts(entering)
    normed = (scaled * gain[...] + shift[...]).astype(BF16)
    lifted = jnp.zeros((rows, width), F32)
    for which in range(3):
        part = slice(which * width, (which + 1) * width)
        piece = grad_qkv[:, part]
        grad = dot_tn(normed, piece).astype(BF16)
        for lanes in range(blocks):
            mixed[which * blocks + lanes] = grad[:, lanes * LANES : (lanes + 1) * LANES]
        lifted = lifted + dot_nt(piece, mixing_in[:, part])
    grad_sent[...] = (gradient + norm_reverse(lifted, scaled, inverse, gain[...])).astype(BF16)
    small[0:1, :] = total_rows(lifted * scaled)
    small[1:2, :] = total_rows(lifted)


def conv_back_kernel(
    numbers, tokens, grad_sent, projected, expanded, slope, active, gain, enlarge, taps, contract,
    grad_in, projector, expander, small, wide_small, grad_cells,
):
    rows, width = projected.shape
    images = rows // SLOTS
    channels = enlarge.shape[1]
    incoming = grad_sent[...].astype(F32)
    scaled, inverse = norm_parts(projected[...])
    proj_low = norm_reverse(incoming, scaled, inverse, gain[...]).astype(BF16)
    small[0:1, :] = total_rows(incoming * scaled)
    small[1:2, :] = total_rows(incoming)
    for start in range(0, channels, BLOCK):
        part = slice(start, start + BLOCK)
        grad = dot_tn(active[:, part], proj_low).astype(BF16)
        for lanes in range(width // LANES):
            projector[lanes, part, :] = grad[:, lanes * LANES : (lanes + 1) * LANES]
    local_in = tokens[...].reshape(rows, width)
    valid = valid_rows(numbers, images)
    column = lax.broadcasted_iota(jnp.int32, (SIDE, LANES), 0)
    first_column, last_column = column == 0, column == SIDE - 1
    total = incoming
    for start in range(0, channels, BLOCK):
        part = slice(start, start + BLOCK)
        grad_conv = dot_nt(proj_low, contract[part, :]) * slope[:, part].astype(F32)
        wide_small[9:10, part] = total_rows(grad_conv)
        grad_cells[...] = grad_conv
        pieces = []
        for lanes in range(0, BLOCK, LANES):
            chans = slice(start + lanes, start + lanes + LANES)
            kernel = [taps[tap : tap + 1, chans] for tap in range(9)]
            sums = [jnp.zeros((SIDE, LANES), F32) for _ in range(9)]
            outcome = []
            for image in range(images):
                base = image * SLOTS
                shifted = {}
                for line in range(SIDE):
                    for ahead in (line, line + 1):
                        if ahead < SIDE and ahead not in shifted:
                            row = grad_cells[
                                base + ahead * SIDE : base + (ahead + 1) * SIDE,
                                lanes : lanes + LANES,
                            ]
                            before, after = column_shifts(row, first_column, last_column)
                            shifted[ahead] = (after, row, before)
                    place = slice(base + line * SIDE, base + (line + 1) * SIDE)
                    cells = expanded[place, chans].astype(F32)
                    grid = jnp.zeros((SIDE, LANES), F32)
                    for a in range(3):
                        if 0 <= line + 1 - a < SIDE:
                            for b in range(3):
                                moved = shifted[line + 1 - a][b]
                                sums[3 * a + b] = sums[3 * a + b] + cells * moved
                                grid = grid + moved * kernel[3 * a + b]
                    outcome.append(grid)
            for tap in range(9):
                wide_small[tap : tap + 1, chans] = total_rows(sums[tap])
            pieces.append(jnp.concatenate(outcome, axis=0) * valid)
        grad_expanded = jnp.concatenate(pieces, axis=1)
        wide_small[10:11, part] = total_rows(grad_expanded)
        expanded_low = grad_expanded.astype(BF16)
        grad = dot_tn(local_in, expanded_low).astype(BF16)
        for lanes in range(BLOCK // LANES):
            expander[start // LANES + lanes] = grad[:, lanes * LANES : (lanes + 1) * LANES]
        total = total + dot_nt(expanded_low, enlarge[:, part])
    grad_in[...] = total.astype(BF16)


WHOLE = pl.BlockSpec(memory_space=pltpu.VMEM)


def call(kernel, name, numbers, ins, outs, scratch=(), tokens=()):
    specs = []
    for place, value in enumerate(ins):
        if place in tokens:
            share = value.shape[0] // 2
            specs.append(
                pl.BlockSpec(
                    (share,) + value.shape[1:], lambda step, numbers: (numbers[0], 0, 0, 0)
                )
            )
        else:
            specs.append(WHOLE)
    return pl.pallas_call(
        kernel if numbers is not None else kernel,
        out_shape=outs,
        grid_spec=pltpu.PrefetchScalarGridSpec(
            num_scalar_prefetch=1,
            grid=(1,),
            in_specs=specs,
            out_specs=[WHOLE] * len(outs),
            scratch_shapes=list(scratch),
        ),
        compiler_params=pltpu.CompilerParams(vmem_limit_bytes=56 * 1024 * 1024),
        name=name,
    )(numbers, *ins)


def shape(dims, kind):
    return jax.ShapeDtypeStruct(dims, kind)


def unpacked(blocks, axis_blocks):
    return jnp.concatenate([blocks[i] for i in range(axis_blocks)], axis=1)


def shards(
    entering_tokens,
    output_sensitivity,
    picture_tile_extents,
    pointwise_enlarge,
    enlarge_bias,
    channelwise_kernel,
    channelwise_conv_bias,
    pointwise_contract,
    convblock_scale,
    convblock_offset,
    attend_scale,
    attend_offset,
    query_key_proj,
    heads_output_proj,
    heads_output_bias,
    feedforward_scale,
    feedforward_offset,
    feedforward_enlarge,
    feedforward_enlarge_bias,
    feedforward_contract,
    contract_bias,
):
    micro_count, local_images, slots, width = entering_tokens.shape
    channels = pointwise_enlarge.shape[1]
    section = lax.axis_index("section")
    share = micro_count // 2
    images = share * local_images
    rows = images * slots
    mine = lax.dynamic_slice_in_dim(picture_tile_extents, section * share, share, 0)
    numbers = jnp.concatenate([section[None].astype(jnp.int32), mine.reshape(-1)])
    line = lambda vector: vector.reshape(1, -1)
    blocks = width // LANES
    wide_blocks = channels // LANES

    sent, expanded, slope, active, projected = call(
        conv_ahead_kernel, "conv_ahead", numbers,
        (entering_tokens, pointwise_enlarge, line(enlarge_bias), channelwise_kernel,
         line(channelwise_conv_bias), pointwise_contract, line(convblock_scale),
         line(convblock_offset)),
        (shape((rows, width), BF16), shape((rows, channels), BF16), shape((rows, channels), BF16),
         shape((rows, channels), BF16), shape((rows, width), F32)),
        [pltpu.VMEM((rows, BLOCK), F32)], (0,),
    )
    qkv, weights, context, middle = call(
        attend_ahead_kernel, "attend_ahead", numbers,
        (sent, line(attend_scale), line(attend_offset), query_key_proj, heads_output_proj,
         line(heads_output_bias)),
        (shape((rows, 3 * width), BF16), shape((images * HEADS, slots, slots), BF16),
         shape((rows, width), BF16), shape((rows, width), F32)),
    )
    output, grad_middle, narrower, widener, mlp_small, mlp_wide = call(
        mlp_kernel, "mlp", numbers,
        (middle, output_sensitivity, line(feedforward_scale), line(feedforward_offset),
         feedforward_enlarge, line(feedforward_enlarge_bias), feedforward_contract,
         line(contract_bias)),
        (shape((rows, width), BF16), shape((rows, width), F32),
         shape((blocks, channels, LANES), BF16), shape((wide_blocks, width, LANES), BF16),
         shape((8, width), F32), shape((1, channels), F32)),
        (), (1,),
    )
    grad_sent, mixed, attend_small = call(
        lambda numbers, *refs: attend_back_kernel(*refs), "attend_back", numbers,
        (sent, grad_middle, qkv, weights, context, line(attend_scale), line(attend_offset),
         query_key_proj, heads_output_proj),
        (shape((rows, width), BF16), shape((4 * blocks, width, LANES), BF16),
         shape((8, width), F32)),
        [pltpu.VMEM((rows, 3 * width), BF16)],
    )
    grad_in, projector, expander, conv_small, conv_wide = call(
        conv_back_kernel, "conv_back", numbers,
        (entering_tokens, grad_sent, projected, expanded, slope, active, line(convblock_scale),
         pointwise_enlarge, channelwise_kernel, pointwise_contract),
        (shape((rows, width), BF16), shape((blocks, channels, LANES), BF16),
         shape((wide_blocks, width, LANES), BF16), shape((8, width), F32),
         shape((16, channels), F32)),
        [pltpu.VMEM((rows, BLOCK), F32)], (0,),
    )

    grads = lax.psum(
        (narrower, widener, mixed, projector, expander, mlp_small, mlp_wide, attend_small,
         conv_small, conv_wide), ("section", "dp")
    )
    narrower, widener, mixed, projector, expander = [g.astype(F32) for g in grads[:5]]
    mlp_small, mlp_wide, attend_small, conv_small, conv_wide = grads[5:]

    own = jnp.stack([grad_in, output]).reshape(2, share, local_images, slots, width)
    first = section == 0
    other = lax.ppermute(jnp.where(first, own[1], own[0]), "section", [(0, 1), (1, 0)])
    ends = jnp.where(
        first,
        jnp.concatenate([own[0], other], axis=0),
        jnp.concatenate([other, own[1]], axis=0),
    )
    squares = jnp.sum(jnp.square(ends.astype(F32)), axis=(2, 3))
    filled = (picture_tile_extents[..., 0] * picture_tile_extents[..., 1]).astype(F32)
    means = jnp.sqrt(squares / (filled * width))
    return (
        ends[None],
        means[None],
        unpacked(expander, wide_blocks),
        conv_wide[10],
        conv_wide[:9],
        conv_wide[9],
        unpacked(projector, blocks),
        conv_small[0],
        conv_small[1],
        attend_small[0],
        attend_small[1],
        unpacked(mixed[: 3 * blocks], 3 * blocks),
        unpacked(mixed[3 * blocks :], blocks),
        mlp_small[3],
        mlp_small[1],
        mlp_small[2],
        unpacked(widener, wide_blocks),
        mlp_wide[0],
        unpacked(narrower, blocks),
        mlp_small[0],
    )


def solution(mesh):
    tokens = P(None, "dp", None, None)
    placed = (tokens, tokens, P(None, "dp", None)) + (P(),) * 18
    return jax.shard_map(
        shards,
        mesh=mesh,
        in_specs=placed,
        out_specs=(P("section", None, "dp", None, None), P("section", None, "dp")) + (P(),) * 18,
        check_vma=False,
    )
```

time: 722 us -> 380 us (0.53); the launches traced: 709 us -> 378 us
  waiting for transfers between devices: 358 us -> 233 us
  other arithmetic: 112 us -> 8.74 us
  matrix products: 89.6 us -> 0 us
  local copies, waits for them, and re-layouts: 113 us -> 24.1 us
  Pallas kernels: 0 us -> 51 us
  blocking collectives: 0 us -> 44.5 us
  loops' own time: 10.3 us -> 0 us
  starting transfers between devices: 10.4 us -> 2.14 us
    psum x2, waiting for transfers between devices: 358 us -> 232 us  [shards(): lax.psum((narrower, widener, mixed, projector, expander, mlp_small, mlp_w...]
    dot_general x24 -> x0, matrix products: 89.6 us -> none  [the longest x8 56.8 us: right_product(): jnp.einsum('na,ba->nb', left, right, preferred_element_type=jnp.float32)]
    pallas_call x0 -> x5, Pallas kernels: none -> 51 us  [call(): pl.pallas_call(kernel if numbers is not None else kernel, out_shape=outs,...]
    reduce_sum x20 -> x1, other arithmetic: 48.6 us -> 0.38 us  [shards(): squares = jnp.sum(jnp.square(ends.astype(F32)), axis=(2, 3))]
    psum x0 -> x1, blocking collectives: none -> 44.5 us  [shards(): lax.psum((narrower, widener, mixed, projector, expander, mlp_small, mlp_w...]
    another operation x100 -> x0, local copies, waits for them, and re-layouts: 41.5 us -> none
    add x13 -> x0, other arithmetic: 28.6 us -> none  [shards(): running + addend]
    unnamed x298 -> x61, local copies, waits for them, and re-layouts: 30.4 us -> 6.16 us
  transfers between devices with their start and end apart: 10 -> 3, of which waited for: 2 -> 2; matrix products, arithmetic and copies ran while one was open for 31% -> 1% of each run, Pallas kernels for 0% -> 0%
where the time goes in v1:
time: 380 us; the launch traced here: 378 us
  waiting for transfers between devices  233 us (61%)
  Pallas kernels  51 us (13%)
  blocking collectives  44.5 us (12%)
  local copies, waits for them, and re-layouts  24.1 us (6%)
  between operations  14.5 us (4%)
  other arithmetic  8.74 us (2%)
    psum x2, waiting for transfers between devices, shards(): lax.psum((narrower, widener, mixed, projector, expander, mlp_small, mlp_w...  232 us
    pallas_call x5, Pallas kernels, call(): pl.pallas_call(kernel if numbers is not None else kernel, out_shape=outs,...  51 us
    psum x1, blocking collectives, shards(): lax.psum((narrower, widener, mixed, projector, expander, mlp_small, mlp_w...  44.5 us
    reshape x11, local copies, waits for them, and re-layouts, shards(): line = lambda vector: vector.reshape(1, -1)  13.8 us
  transfers between devices with their start and end apart: 3, of which 2 were waited for; matrix products, arithmetic and copies ran while one was open for 1% of the time, Pallas kernels for 0%

profile of v1, /device:TPU:1, one launch (start us, length us, event | category | flops | bytes accessed | tf_op | source)
XLA Modules:
  0.0 377.9 jit_solution(1964527922207915804)
XLA Ops:
  7.2 0.8 constant_dynamic-slice_fusion
  8.2 1.2 reshape.293.gain
  9.4 1.3 reshape.291.enlarge_bias
  10.7 1.3 reshape.292.taps_bias
  12.0 1.2 reshape.294.shift
  13.3 1.2 reshape.295.gain.refs_5_
  14.5 1.2 reshape.296.shift.refs_6_
  15.7 1.2 reshape.297.mixing_bias
  17.0 1.3 reshape.300.enlarge_bias
  18.3 1.2 reshape.298.gain
  19.5 1.2 reshape.299.shift
  20.8 1.2 reshape.301.contract_bias
  22.6 10.1 %conv_ahead.1 = (bf16[512,384]{1,0:T(8,128)(2,1)}, bf16[512,1536]{1,0:T(8,128)(2,1)}, bf16[512,1536]{1,0:T(8,128)(2,1)}, bf16[512,1536]{1,0:T(8,128)(2,1)}, f32[512,384]{1,0:T(8,128)}) custom-call(s32[5]{0:T(128)} %pad_add_fusion.numbers, bf16[4,1,256,384]{3,2,1,0:T(8,128)(2,1)} %tokens.3, bf16[384,1536]{1,0:T(8,128)(2,1)} %enlarge.5, ...), custom_call_target="tpu_custom_call" | custom-call | tf_op jit(solution)/shard_map/conv_ahead/pallas_call | solution.py:343
  32.7 6.1 %attend_ahead.1 = (bf16[512,1152]{1,0:T(8,128)(2,1)}, bf16[12,256,256]{2,1,0:T(8,128)(2,1)}, bf16[512,384]{1,0:T(8,128)(2,1)}, f32[512,384]{1,0:T(8,128)}) custom-call(s32[5]{0:T(128)} %pad_add_fusion.numbers, bf16[512,384]{1,0:T(8,128)(2,1)} %get-tuple-element.43.sent.refs_0_, f32[1,384]{1,0:T(1,128)} %reshape.295.gain.refs_5_, ...), custom_call_target="tpu_custom_call" | custom-call | tf_op jit(solution)/shard_map/attend_ahead/pallas_call | solution.py:343
  38.8 10.0 %mlp.1 = (bf16[512,384]{1,0:T(8,128)(2,1)}, f32[512,384]{1,0:T(8,128)}, bf16[3,1536,128]{2,1,0:T(8,128)(2,1)}, bf16[12,384,128]{2,1,0:T(8,128)(2,1)}, f32[8,384]{1,0:T(8,128)}, /*index=5*/f32[1,1536]{1,0:T(1,128)}) custom-call(s32[5]{0:T(128)} %pad_add_fusion.numbers, f32[512,384]{1,0:T(8,128)} %get-tuple-element.44.middle, ...), custom_call_target="tpu_custom_call" | custom-call | tf_op jit(solution)/shard_map/mlp/pallas_call | solution.py:343
  48.9 9.9 %attend_back.1 = (bf16[512,384]{1,0:T(8,128)(2,1)}, bf16[12,384,128]{2,1,0:T(8,128)(2,1)}, f32[8,384]{1,0:T(8,128)}) custom-call(s32[5]{0:T(128)} %pad_add_fusion.numbers, bf16[512,384]{1,0:T(8,128)(2,1)} %get-tuple-element.43.sent.refs_0_, f32[512,384]{1,0:T(8,128)} %get-tuple-element.45.refs_1_, bf16[512,1152]{1,0:T(8,128)(2,1)} %get-tuple-element.46.refs_2_, ...), custom_call_target="tpu_custom_call" | custom-call | tf_op jit(solution)/shard_map/attend_back/pallas_call | solution.py:343
  58.8 14.9 %conv_back.1 = (bf16[512,384]{1,0:T(8,128)(2,1)}, bf16[3,1536,128]{2,1,0:T(8,128)(2,1)}, bf16[12,384,128]{2,1,0:T(8,128)(2,1)}, f32[8,384]{1,0:T(8,128)}, f32[16,1536]{1,0:T(8,128)}) custom-call(s32[5]{0:T(128)} %pad_add_fusion.numbers, bf16[4,1,256,384]{3,2,1,0:T(8,128)(2,1)} %tokens.3, bf16[512,384]{1,0:T(8,128)(2,1)} %get-tuple-element.49.grad_sent, ...), custom_call_target="tpu_custom_call" | custom-call | tf_op jit(solution)/shard_map/conv_back/pallas_call | solution.py:343
  73.8 0.6 all-reduce.7.cloned.1.call-update
  74.9 2.1 collective-permute-start
  77.0 44.5 %all-reduce = (f32[8,384]{1,0:T(8,128)S(1)}, f32[8,384]{1,0:T(8,128)S(1)}, f32[8,384]{1,0:T(8,128)S(1)}, f32[1536]{0:T(1024)}) all-reduce(f32[8,384]{1,0:T(8,128)S(1)} %copy-done.12, f32[8,384]{1,0:T(8,128)S(1)} %copy-done.11, f32[8,384]{1,0:T(8,128)S(1)} %copy-done.10, ...), channel_id=1, replica_groups=mesh['section'=2,'dp'=16] {'section','dp'}, use_global_device_ids=true, to_apply=%region_4.0 | all-reduce | flops 10752 | bytes 86016 | tf_op jit(solution)/shard_map/psum | solution.py:445
  122.7 73.6 %all-reduce.5.cloned.1.call-done = f32[16,1536]{1,0:T(8,128)} async-done(((f32[16,1536]{1,0:T(8,128)}), f32[16,1536]{1,0:T(8,128)}) %all-reduce.5.cloned.1.call-update) | async-done | bytes 98320 | tf_op jit(solution)/shard_map/psum | solution.py:445
  196.3 1.5 slice_reduce_fusion
  198.2 1.0 maximum_select_fusion
  199.8 158.6 %all-reduce.7.cloned.1.call-done = (bf16[12,384,128]{2,1,0:T(8,128)(2,1)}, bf16[3,1536,128]{2,1,0:T(8,128)(2,1)}, bf16[12,384,128]{2,1,0:T(8,128)(2,1)}, bf16[12...) async-done(((bf16[12,384,128]{2,1,0:T(8,128)(2,1)}, bf16[3,1536,128]{2,1,0:T(8,128)(2,1)}, bf16[12,384,128]{2,1,0:T(8,128)(2,1)}, bf16[12,384,128]{2,1,0:T(8,128)(2,1)}, ...) | async-done | bytes 5898256 | tf_op jit(solution)/shard_map/psum | solution.py:445
  358.4 1.5 convert_element_type.43
  360.1 1.0 copy-done.5
  361.7 1.0 copy-done.4
  363.0 1.1 copy-done.3
  364.4 1.1 copy-done.2
  366.1 0.9 pad_maximum_fusion.2
  367.1 3.0 pad_maximum_fusion
  370.4 0.6 copy.80
  (78 shorter events, 5.5 us)
Async XLA Ops:
  7.2 189.1 %all-reduce.5.cloned.1.call-start = ((), (), s32[]{:S(2)}) async-start(), calls=%async_computation | async-start | bytes 196608 | tf_op jit(solution)/shard_map/psum | solution.py:445
  73.7 284.7 %all-reduce.7.cloned.1.call-start = ((), (), s32[]{:S(2)}) async-start(), calls=%async_computation.1 | async-start | bytes 11796480 | tf_op jit(solution)/shard_map/psum | solution.py:445
  73.7 1.0 copy-start
  73.7 1.1 copy-start.1
  73.7 3.2 copy-start.13
  73.8 3.2 copy-start.10
  73.8 3.2 copy-start.11
  73.8 3.2 copy-start.12
  74.4 124.8 %copy-start.14 = (s32[4,1,2]{0,2,1:T(2,128)S(1)}, s32[4,1,2]{0,2,1:T(2,128)}, u32[]{:S(2)}) copy-start(s32[4,1,2]{0,2,1:T(2,128)} %param.23) | copy-start | bytes 100
  74.9 122.9 %collective-permute-start = (bf16[2,1,256,384]{3,2,0,1:T(8,128)(2,1)S(1)}, bf16[2,1,256,384]{3,2,0,1:T(8,128)(2,1)S(1)}, u32[]{:S(2)}, u32[]{:S(2)}) collective-permute-start(bf16[2,1,256,384]{3,2,0,1:T(8,128)(2,1)S(1)} %broadcast_select_fusion), channel_id=1, source_target_pairs={{0,16},{16,0},{1,17},{17,1},{2,18},{18,2},{3,19},{19,3},{4,20},{20... | collective-permute-start | bytes 1179656 | tf_op jit(solution)/shard_map/ppermute | solution.py:454
  359.9 1.3 copy-start.5
  361.4 1.3 copy-start.4
  362.8 1.3 copy-start.3
  364.2 1.3 copy-start.2
  366.0 4.0 %copy-start.9 = (f32[384,1536]{1,0:T(8,128)}, f32[384,1536]{1,0:T(8,128)S(1)}, u32[]{:S(2)}) copy-start(f32[384,1536]{1,0:T(8,128)S(1)} %fusion.21) | copy-start | bytes 7077892
  366.1 4.0 %copy-start.7 = (f32[384,1152]{1,0:T(8,128)}, f32[384,1152]{1,0:T(8,128)S(1)}, u32[]{:S(2)}) copy-start(f32[384,1152]{1,0:T(8,128)S(1)} %get-tuple-element.111) | copy-start | bytes 5308420
  366.1 4.3 %copy-start.8 = (f32[384,1536]{1,0:T(8,128)}, f32[384,1536]{1,0:T(8,128)S(1)}, u32[]{:S(2)}) copy-start(f32[384,1536]{1,0:T(8,128)S(1)} %get-tuple-element.116) | copy-start | bytes 7077892
  367.0 3.3 copy-start.6
Sparse Core Ops, SparseCore 0:
  73.8 122.4 all-reduce.4
  203.3 155.0 all-reduce.6
